TPU v7x, 1024 devices: a whole 4x8x16 slice. The times are simulated.
1024 devices in a mesh: blk: 16 (over x, y_lo, core), dp: 64 (over z, y_hi).
Axes of the slice: x: 4, y: 8 (y_hi: 4, y_lo: 2; y = y_hi * 2 + y_lo), z: 16, core: 2. Of those that a mesh axis runs over, the one named last changes fastest.
Arguments:
- patches: bfloat16 [16, 64, 64, 12, 1152], P('blk', 'dp'), may hold values from -8 to 8
- counts: int32 [16, 64, 64], P('blk'), may hold values from 0 to 12, as said below
- w_qkv: bfloat16 [1152, 1728], replicated, may hold values from -0.1875 to 0.1875
- w_out: bfloat16 [576, 1152], replicated, may hold values from -0.25 to 0.25
- text_rows: bfloat16 [64, 768, 1152], P('dp', 'blk'), may hold values from -160 to 160
- labels: int32 [64, 768], P('dp', 'blk'), may hold values from 0 to 767, each once within a row
Outputs:
- losses: float32 [64, 768], P('dp', 'blk')
- d_pooled: float32 [64, 768, 1152], P('dp', 'blk')
- d_texts: float32 [64, 768, 1152], P('dp', 'blk')
Inputs may be any that keep to these rules, and one draw needn't show every extreme that they name: `counts`: A device sends at most one image to each device of its dp group; every device receives exactly 48 images with exactly 384 patches in all, and one of them has exactly 12 patches; a sent image has at least 4 patches. `labels`: each row is a permutation of the group's text indices.
All inputs are finite; a program needn't handle non-finite values.
Results may differ from a plain program's by a relative error of at most 0.0046.
Values may be sent and summed in bfloat16 or wider, within the bound.
A program may use at most 64 MiB of HBM per device.

v0:
```python
import jax
import jax.numpy as jnp
from jax import lax
from jax.sharding import PartitionSpec as P

HEADS = 8
HEAD_DIM = 72


logit_scale = 16.0
logit_bias = -4.0
epsilon = 1e-06
highest = lax.Precision.HIGHEST


def from_behind(value, axis, steps):
    count = lax.axis_size(axis)
    pairs = [(source, (source + steps) % count) for source in range(count)]
    return lax.ppermute(value, axis, pairs)


def normalize_rows(values):
    scaling = lax.rsqrt(jnp.sum(values * values, axis=-1, keepdims=True) + epsilon)
    return (values * scaling, scaling)


def normalize_tokens(row_block):
    widened = row_block.astype(jnp.float32)
    centred = widened - jnp.mean(widened, axis=-1, keepdims=True)
    spread = jnp.mean(centred * centred, axis=-1, keepdims=True)
    return (widened, (centred * lax.rsqrt(spread + epsilon)).astype(jnp.bfloat16))


def project_heads(normed, w_qkv):
    packed = jnp.dot(normed, w_qkv, preferred_element_type=jnp.float32).astype(jnp.bfloat16)
    inner_width = HEADS * HEAD_DIM
    leading = normed.shape[0]
    query_rows = packed[:, :inner_width].reshape(leading, HEADS, HEAD_DIM)
    key_rows = packed[:, inner_width : 2 * inner_width].reshape(leading, HEADS, HEAD_DIM)
    value_rows = packed[:, 2 * inner_width :].reshape(leading, HEADS, HEAD_DIM)
    return (query_rows, key_rows, value_rows)


def pool_blocks(image_rows, image_lengths, w_qkv, w_out):
    targets, cap_rows, feature_count = image_rows.shape
    widened, normed = normalize_tokens(image_rows.reshape(targets * cap_rows, feature_count))
    query_rows, key_rows, value_rows = project_heads(normed, w_qkv)
    query_rows = query_rows.reshape(targets, cap_rows, HEADS, HEAD_DIM)
    key_rows = key_rows.reshape(targets, cap_rows, HEADS, HEAD_DIM)
    value_rows = value_rows.reshape(targets, cap_rows, HEADS, HEAD_DIM)
    scores = jnp.einsum(
        "bqhd,bkhd->bhqk", query_rows, key_rows, preferred_element_type=jnp.float32
    ) * HEAD_DIM ** (-0.5)
    usable = jnp.arange(cap_rows, dtype=jnp.int32)[None, :] < image_lengths[:, None]
    raised = jnp.where(usable[:, None, None, :], jnp.exp(scores), 0.0)
    denominators = (
        jnp.sum(raised, axis=-1, keepdims=True)
        + jnp.where(image_lengths > 0, 0.0, 1.0)[:, None, None, None]
    )
    weights = (raised / denominators).astype(jnp.bfloat16)
    mixed_heads = jnp.einsum(
        "bhqk,bkhd->bqhd", weights, value_rows, preferred_element_type=jnp.float32
    )
    mixed_heads = mixed_heads.astype(jnp.bfloat16).reshape(targets * cap_rows, HEADS * HEAD_DIM)
    result = widened + jnp.dot(mixed_heads, w_out, preferred_element_type=jnp.float32)
    result = result.reshape(targets, cap_rows, feature_count)
    kept_rows = usable.astype(jnp.float32)[:, :, None]
    totals = jnp.sum(result * kept_rows, axis=1)
    return totals / jnp.maximum(image_lengths, 1).astype(jnp.float32)[:, None]


def pair_terms(unit_img, text_block, label_rows, first_column):
    text_unit, text_scale = normalize_rows(text_block.astype(jnp.float32))
    logits = (
        logit_scale * jnp.einsum("id,jd->ij", unit_img, text_unit, precision=highest) + logit_bias
    )
    columns = first_column + jnp.arange(text_block.shape[0], dtype=jnp.int32)
    signed = jnp.where(label_rows[:, None] == columns[None, :], 1.0, -1.0)
    losses = jnp.sum(jax.nn.softplus(-signed * logits), axis=1)
    slopes = -signed * jax.nn.sigmoid(-signed * logits)
    return (text_unit, losses, slopes)


def local(patches, counts, w_qkv, w_out, text_rows, labels):
    group_size = lax.axis_size("dp")
    own_place = lax.axis_index("dp")
    count_table = counts[0]
    places = jnp.arange(group_size, dtype=jnp.int32)
    intake = jnp.sum(jnp.where(places[None, :] == own_place, count_table, 0), axis=1)
    label_rows = labels[0]
    image_count = label_rows.shape[0]
    living = (intake > 0).astype(jnp.int32)
    ranking = jnp.cumsum(living) - living
    chooser = (
        (living[None, :] == 1)
        & (ranking[None, :] == jnp.arange(image_count, dtype=jnp.int32)[:, None])
    ).astype(jnp.int32)
    arrived = lax.all_to_all(patches[0, 0], "dp", split_axis=0, concat_axis=0, tiled=True)
    source_pick = jnp.sum(chooser * places[None, :], axis=1)
    image_lengths = jnp.sum(chooser * intake[None, :], axis=1)
    image_rows = jnp.take(arrived, source_pick, axis=0)
    pooled = pool_blocks(image_rows, image_lengths, w_qkv, w_out)
    unit_img, img_scale = normalize_rows(pooled)
    text_block = text_rows[0]
    blk_count = lax.axis_size("blk")
    own_turn = lax.axis_index("blk")

    def one_turn(turn_index, carried):
        held_block, carried_grads, loss_sums, unit_grads = carried
        anchor = (own_turn - turn_index) % blk_count
        text_unit, new_losses, slopes = pair_terms(
            unit_img, held_block, label_rows, anchor * image_count
        )
        loss_sums = loss_sums + new_losses
        unit_grads = unit_grads + logit_scale * jnp.einsum(
            "ij,jd->id", slopes, text_unit, precision=highest
        )
        carried_grads = carried_grads + logit_scale * jnp.einsum(
            "ij,id->jd", slopes, unit_img, precision=highest
        )
        held_block = from_behind(held_block, "blk", 1)
        carried_grads = from_behind(carried_grads, "blk", 1)
        return (held_block, carried_grads, loss_sums, unit_grads)

    starting = (
        text_block,
        jnp.zeros(text_block.shape, jnp.float32),
        jnp.zeros((image_count,), jnp.float32),
        jnp.zeros(pooled.shape, jnp.float32),
    )
    held_block, grad_text, losses, grad_img = lax.fori_loop(0, blk_count, one_turn, starting)
    own_unit, own_scale = normalize_rows(text_block.astype(jnp.float32))
    d_texts = (
        grad_text - own_unit * jnp.sum(own_unit * grad_text, axis=-1, keepdims=True)
    ) * own_scale
    d_pooled = (
        grad_img - unit_img * jnp.sum(unit_img * grad_img, axis=-1, keepdims=True)
    ) * img_scale
    return (losses[None], d_pooled[None], d_texts[None])


def solution(mesh):
    in_specs = (
        P("blk", "dp", None, None, None),
        P("blk", None, None),
        P(),
        P(),
        P("dp", "blk", None),
        P("dp", "blk"),
    )
    out_specs = (P("dp", "blk"), P("dp", "blk", None), P("dp", "blk", None))
    return jax.shard_map(local, mesh=mesh, in_specs=in_specs, out_specs=out_specs, check_vma=False)
```

profile of v0, /device:TPU:1, one launch (start us, length us, event | category | flops | bytes accessed | tf_op | source)
XLA Modules:
  0.0 386.7 jit_solution(14402404143684646851)
XLA Ops:
  0.6 4.0 %copy.47 = bf16[1,1,64,12,1152]{4,3,2,1,0:T(8,128)(2,1)} copy(bf16[1,1,64,12,1152]{4,2,3,1,0:T(8,128)(2,1)} %param.8) | data formatting | bytes 3538944 | tf_op args[0]
  4.6 25.9 %all-to-all-start = ((bf16[64,12,1152]{2,1,0:T(8,128)(2,1)}), bf16[64,12,1152]{2,1,0:T(8,128)(2,1)}, u32[]{:S(2)}, u32[]{:S(2)}) async-start(bf16[64,12,1152]{2,1,0:T(8,128)(2,1)} %bitcast.43), calls=%async_computation | async-start | bytes 4718592 | tf_op jit(solution)/shard_map/all_to_all | solution.py:98
  34.0 102.8 %all-to-all-done = bf16[64,12,1152]{2,1,0:T(8,128)(2,1)} async-done(((bf16[64,12,1152]{2,1,0:T(8,128)(2,1)}), bf16[64,12,1152]{2,1,0:T(8,128)(2,1)}, u32[]{:S(2)}, u32[]{:S(2)}) %all-to-all-start) | async-done | bytes 1769504 | tf_op jit(solution)/shard_map/all_to_all | solution.py:98
  136.8 2.5 gather_fusion
  145.5 5.6 %convolution_convert_fusion = bf16[576,1728]{1,0:T(8,128)(2,1)S(1)} fusion(bf16[1152,1728]{0,1:T(8,128)(2,1)} %param.10, f32[576]{0:T(1024)S(1)} %rsqrt.43, f32[576]{0:T(1024)S(1)} %div.35, bf16[576,1152]{1,0:T(8,128)(2,1)} %gather.7, pred[576]{0:T(1024)(128)(4,1)} %broadcast_in_dim.111), kind=kOutput, calls=%fused_computation.29 | convolution fusion | flops 2297548800 | bytes 7304256 | tf_op jit(solution)/shard_map/dot_general | solution.py:35
  152.9 2.3 reshape_reshape.10
  155.2 3.1 reshape_reshape.11
  158.3 3.9 %fusion.15 = f32[48,8,12,12]{2,3,1,0:T(8,128)} fusion(bf16[48,12,8,72]{3,2,1,0:T(8,128)(2,1)} %reshape_reshape.11, bf16[48,12,8,72]{3,2,1,0:T(8,128)(2,1)S(1)} %reshape_reshape.10), kind=kOutput, calls=%fused_computation.36 | convolution fusion | flops 7962624 | bytes 1548288 | tf_op jit(solution)/shard_map/bqhd,bkhd->bhqk/dot_general | solution.py:51
  162.2 3.2 copy.33
  165.8 4.1 %copy.35 = bf16[48,8,12,12]{3,2,1,0:T(8,128)(2,1)} copy(bf16[48,8,12,12]{0,1,3,2:T(8,128)(2,1)S(1)} %divide_convert_fusion) | data formatting | bytes 221184 | tf_op jit(solution)/shard_map/convert_element_type | solution.py:60
  169.9 2.5 reshape_reshape.9
  172.4 2.0 fusion.18
  176.6 4.3 %convolution_add_fusion = f32[576,1152]{1,0:T(8,128)} fusion(bf16[576,576]{1,0:T(8,128)(2,1)} %reshape.206, bf16[576,1152]{1,0:T(8,128)(2,1)S(1)} %copy-done, bf16[576,1152]{1,0:T(8,128)(2,1)} %gather.7, pred[576]{0:T(1024)(128)(4,1)S(1)} %copy-done.10), kind=kOutput, calls=%fused_computation.24 | convolution fusion | flops 766402560 | bytes 5972544 | tf_op jit(solution)/shard_map/dot_general | solution.py:65
  180.9 4.0 %reshape.207 = f32[48,12,1152]{2,1,0:T(8,128)} reshape(f32[576,1152]{1,0:T(8,128)} %convolution_add_fusion) | data formatting | bytes 5308416 | tf_op jit(solution)/shard_map/reshape | solution.py:66
  184.9 2.9 multiply_reduce_fusion
  188.2 196.6 %while.22 = (s32[]{:T(128)}, bf16[48,1152]{1,0:T(8,128)(2,1)S(1)}, f32[48,1152]{1,0:T(8,128)S(1)}, f32[48]{0:T(128)S(1)}, f32[48,1152]{1,0:T(8,128)S(1)}, /*inde...) while((s32[]{:T(128)}, bf16[48,1152]{1,0:T(8,128)(2,1)S(1)}, ...), condition=%wide.region_12.13_spmd.clone, body=%wide.region_9.12_spmd.clone.sunk | while | flops 96277360 | bytes 3238241 | solution.py:131
  188.2 8.3 %collective-permute-start = (bf16[48,1152]{1,0:T(8,128)(2,1)S(1)}, bf16[48,1152]{1,0:T(8,128)(2,1)S(1)}, u32[]{:S(2)}, u32[]{:S(2)}) collective-permute-start(bf16[48,1152]{1,0:T(8,128)(2,1)S(1)} %copy.54), channel_id=1, source_target_pairs={{0,64},{64,128},{128,192},{192,256},{256,320},{320,384},{384,448},... | collective-permute-start | bytes 331784 | tf_op jit(solution)/shard_map/while/body/eval_jaxpr/ppermute | solution.py:19
  197.5 1.9 collective-permute-start.1
  200.0 2.3 collective-permute-done.1
  202.3 4.4 %collective-permute-start = (bf16[48,1152]{1,0:T(8,128)(2,1)S(1)}, bf16[48,1152]{1,0:T(8,128)(2,1)S(1)}, u32[]{:S(2)}, u32[]{:S(2)}) collective-permute-start(bf16[48,1152]{1,0:T(8,128)(2,1)S(1)} %copy.54), channel_id=1, source_target_pairs={{0,64},{64,128},{128,192},{192,256},{256,320},{320,384},{384,448},... | collective-permute-start | bytes 331784 | tf_op jit(solution)/shard_map/while/body/eval_jaxpr/ppermute | solution.py:19
  207.7 1.9 collective-permute-start.1
  210.2 2.3 collective-permute-done.1
  212.5 4.4 %collective-permute-start = (bf16[48,1152]{1,0:T(8,128)(2,1)S(1)}, bf16[48,1152]{1,0:T(8,128)(2,1)S(1)}, u32[]{:S(2)}, u32[]{:S(2)}) collective-permute-start(bf16[48,1152]{1,0:T(8,128)(2,1)S(1)} %copy.54), channel_id=1, source_target_pairs={{0,64},{64,128},{128,192},{192,256},{256,320},{320,384},{384,448},... | collective-permute-start | bytes 331784 | tf_op jit(solution)/shard_map/while/body/eval_jaxpr/ppermute | solution.py:19
  217.9 2.7 collective-permute-start.1
  221.7 3.1 collective-permute-done.1
  224.8 3.1 collective-permute-start
  228.9 2.8 collective-permute-start.1
  234.0 3.1 collective-permute-done.1
  237.1 1.9 collective-permute-start
  240.0 2.8 collective-permute-start.1
  243.4 2.9 collective-permute-done
  246.3 3.1 collective-permute-done.1
  249.4 1.9 collective-permute-start
  252.3 1.9 collective-permute-start.1
  254.8 3.8 collective-permute-done
  258.6 3.1 collective-permute-done.1
  261.7 1.9 collective-permute-start
  264.7 1.9 collective-permute-start.1
  267.1 3.8 collective-permute-done
  270.9 3.1 collective-permute-done.1
  274.0 1.9 collective-permute-start
  279.4 3.8 collective-permute-done
  283.2 3.1 collective-permute-done.1
  289.3 1.9 collective-permute-start.1
  291.7 3.8 collective-permute-done
  295.5 3.1 collective-permute-done.1
  304.0 3.8 collective-permute-done
  307.9 3.1 collective-permute-done.1
  316.3 3.8 collective-permute-done
  320.2 3.1 collective-permute-done.1
  326.2 1.9 collective-permute-start.1
  328.7 3.8 collective-permute-done
  332.5 3.1 collective-permute-done.1
  341.0 3.8 collective-permute-done
  344.8 3.1 collective-permute-done.1
  350.8 1.9 collective-permute-start.1
  353.3 3.8 collective-permute-done
  357.1 3.1 collective-permute-done.1
  360.2 1.9 collective-permute-start
  365.6 3.8 collective-permute-done
  369.4 3.1 collective-permute-done.1
  375.5 1.9 collective-permute-start.1
  377.9 3.8 collective-permute-done
  381.7 3.1 collective-permute-done.1
  (210 shorter events, 64.6 us)
Async XLA Ops:
  0.6 176.0 %copy-start = (bf16[576,1152]{1,0:T(8,128)(2,1)S(1)}, bf16[576,1152]{1,0:T(8,128)(2,1)}, u32[]{:S(2)}) copy-start(bf16[576,1152]{1,0:T(8,128)(2,1)} %param.11) | copy-start | bytes 3981316
  4.6 26.0 %copy-start.5 = (s32[1,64,64]{2,1,0:T(8,128)S(1)}, s32[1,64,64]{2,1,0:T(8,128)}, u32[]{:S(2)}) copy-start(s32[1,64,64]{2,1,0:T(8,128)} %param.9) | copy-start | bytes 49156
  4.6 28.1 %copy-start.1 = (bf16[1,48,1152]{2,1,0:T(8,128)(2,1)S(1)}, bf16[1,48,1152]{2,1,0:T(8,128)(2,1)}, u32[]{:S(2)}) copy-start(bf16[1,48,1152]{2,1,0:T(8,128)(2,1)} %param.12) | copy-start | bytes 331780
  4.6 132.1 %all-to-all-start = ((bf16[64,12,1152]{2,1,0:T(8,128)(2,1)}), bf16[64,12,1152]{2,1,0:T(8,128)(2,1)}, u32[]{:S(2)}, u32[]{:S(2)}) async-start(bf16[64,12,1152]{2,1,0:T(8,128)(2,1)} %bitcast.43), calls=%async_computation | async-start | bytes 4718592 | tf_op jit(solution)/shard_map/all_to_all | solution.py:98
  31.2 0.8 copy-start.7
  139.3 1.9 copy-start.8
  140.5 0.6 copy-start.2
  162.2 3.4 copy-start.11
  174.4 2.2 copy-start.10
  180.9 4.0 %copy-start.4 = (f32[48,12]{1,0:T(8,128)S(1)}, f32[48,12]{1,0:T(8,128)}, u32[]{:S(2)}) copy-start(f32[48,12]{1,0:T(8,128)} %copy.37) | copy-start | bytes 6916
  184.9 3.3 copy-start.3
  188.2 196.6 %copy-start.9 = (f32[48]{0:T(128)S(1)}, f32[48]{0:T(128)}, u32[]{:S(2)}) copy-start(f32[48]{0:T(128)} %add_rsqrt_fusion.2) | copy-start | bytes 580
  188.2 11.8 %collective-permute-start = (bf16[48,1152]{1,0:T(8,128)(2,1)S(1)}, bf16[48,1152]{1,0:T(8,128)(2,1)S(1)}, u32[]{:S(2)}, u32[]{:S(2)}) collective-permute-start(bf16[48,1152]{1,0:T(8,128)(2,1)S(1)} %copy.54), channel_id=1, source_target_pairs={{0,64},{64,128},{128,192},{192,256},{256,320},{320,384},{384,448},... | collective-permute-start | bytes 331784 | tf_op jit(solution)/shard_map/while/body/eval_jaxpr/ppermute | solution.py:19
  197.5 4.8 %collective-permute-start.1 = (f32[48,1152]{1,0:T(8,128)S(1)}, f32[48,1152]{1,0:T(8,128)S(1)}, u32[]{:S(2)}, u32[]{:S(2)}) collective-permute-start(f32[48,1152]{1,0:T(8,128)S(1)} %fusion.57), channel_id=1, source_target_pairs={{0,64},{64,128},{128,192},{192,256},{256,320},{320,384},{384,448},... | collective-permute-start | bytes 663560 | tf_op jit(solution)/shard_map/while/body/eval_jaxpr/ppermute | solution.py:19
  202.3 7.9 %collective-permute-start = (bf16[48,1152]{1,0:T(8,128)(2,1)S(1)}, bf16[48,1152]{1,0:T(8,128)(2,1)S(1)}, u32[]{:S(2)}, u32[]{:S(2)}) collective-permute-start(bf16[48,1152]{1,0:T(8,128)(2,1)S(1)} %copy.54), channel_id=1, source_target_pairs={{0,64},{64,128},{128,192},{192,256},{256,320},{320,384},{384,448},... | collective-permute-start | bytes 331784 | tf_op jit(solution)/shard_map/while/body/eval_jaxpr/ppermute | solution.py:19
  207.7 4.8 %collective-permute-start.1 = (f32[48,1152]{1,0:T(8,128)S(1)}, f32[48,1152]{1,0:T(8,128)S(1)}, u32[]{:S(2)}, u32[]{:S(2)}) collective-permute-start(f32[48,1152]{1,0:T(8,128)S(1)} %fusion.57), channel_id=1, source_target_pairs={{0,64},{64,128},{128,192},{192,256},{256,320},{320,384},{384,448},... | collective-permute-start | bytes 663560 | tf_op jit(solution)/shard_map/while/body/eval_jaxpr/ppermute | solution.py:19
  212.5 9.1 %collective-permute-start = (bf16[48,1152]{1,0:T(8,128)(2,1)S(1)}, bf16[48,1152]{1,0:T(8,128)(2,1)S(1)}, u32[]{:S(2)}, u32[]{:S(2)}) collective-permute-start(bf16[48,1152]{1,0:T(8,128)(2,1)S(1)} %copy.54), channel_id=1, source_target_pairs={{0,64},{64,128},{128,192},{192,256},{256,320},{320,384},{384,448},... | collective-permute-start | bytes 331784 | tf_op jit(solution)/shard_map/while/body/eval_jaxpr/ppermute | solution.py:19
  217.9 6.8 %collective-permute-start.1 = (f32[48,1152]{1,0:T(8,128)S(1)}, f32[48,1152]{1,0:T(8,128)S(1)}, u32[]{:S(2)}, u32[]{:S(2)}) collective-permute-start(f32[48,1152]{1,0:T(8,128)S(1)} %fusion.57), channel_id=1, source_target_pairs={{0,64},{64,128},{128,192},{192,256},{256,320},{320,384},{384,448},... | collective-permute-start | bytes 663560 | tf_op jit(solution)/shard_map/while/body/eval_jaxpr/ppermute | solution.py:19
  224.8 9.2 %collective-permute-start = (bf16[48,1152]{1,0:T(8,128)(2,1)S(1)}, bf16[48,1152]{1,0:T(8,128)(2,1)S(1)}, u32[]{:S(2)}, u32[]{:S(2)}) collective-permute-start(bf16[48,1152]{1,0:T(8,128)(2,1)S(1)} %copy.54), channel_id=1, source_target_pairs={{0,64},{64,128},{128,192},{192,256},{256,320},{320,384},{384,448},... | collective-permute-start | bytes 331784 | tf_op jit(solution)/shard_map/while/body/eval_jaxpr/ppermute | solution.py:19
  228.9 8.1 %collective-permute-start.1 = (f32[48,1152]{1,0:T(8,128)S(1)}, f32[48,1152]{1,0:T(8,128)S(1)}, u32[]{:S(2)}, u32[]{:S(2)}) collective-permute-start(f32[48,1152]{1,0:T(8,128)S(1)} %fusion.57), channel_id=1, source_target_pairs={{0,64},{64,128},{128,192},{192,256},{256,320},{320,384},{384,448},... | collective-permute-start | bytes 663560 | tf_op jit(solution)/shard_map/while/body/eval_jaxpr/ppermute | solution.py:19
  237.1 9.2 %collective-permute-start = (bf16[48,1152]{1,0:T(8,128)(2,1)S(1)}, bf16[48,1152]{1,0:T(8,128)(2,1)S(1)}, u32[]{:S(2)}, u32[]{:S(2)}) collective-permute-start(bf16[48,1152]{1,0:T(8,128)(2,1)S(1)} %copy.54), channel_id=1, source_target_pairs={{0,64},{64,128},{128,192},{192,256},{256,320},{320,384},{384,448},... | collective-permute-start | bytes 331784 | tf_op jit(solution)/shard_map/while/body/eval_jaxpr/ppermute | solution.py:19
  240.0 9.3 %collective-permute-start.1 = (f32[48,1152]{1,0:T(8,128)S(1)}, f32[48,1152]{1,0:T(8,128)S(1)}, u32[]{:S(2)}, u32[]{:S(2)}) collective-permute-start(f32[48,1152]{1,0:T(8,128)S(1)} %fusion.57), channel_id=1, source_target_pairs={{0,64},{64,128},{128,192},{192,256},{256,320},{320,384},{384,448},... | collective-permute-start | bytes 663560 | tf_op jit(solution)/shard_map/while/body/eval_jaxpr/ppermute | solution.py:19
  249.4 9.2 %collective-permute-start = (bf16[48,1152]{1,0:T(8,128)(2,1)S(1)}, bf16[48,1152]{1,0:T(8,128)(2,1)S(1)}, u32[]{:S(2)}, u32[]{:S(2)}) collective-permute-start(bf16[48,1152]{1,0:T(8,128)(2,1)S(1)} %copy.54), channel_id=1, source_target_pairs={{0,64},{64,128},{128,192},{192,256},{256,320},{320,384},{384,448},... | collective-permute-start | bytes 331784 | tf_op jit(solution)/shard_map/while/body/eval_jaxpr/ppermute | solution.py:19
  252.3 9.4 %collective-permute-start.1 = (f32[48,1152]{1,0:T(8,128)S(1)}, f32[48,1152]{1,0:T(8,128)S(1)}, u32[]{:S(2)}, u32[]{:S(2)}) collective-permute-start(f32[48,1152]{1,0:T(8,128)S(1)} %fusion.57), channel_id=1, source_target_pairs={{0,64},{64,128},{128,192},{192,256},{256,320},{320,384},{384,448},... | collective-permute-start | bytes 663560 | tf_op jit(solution)/shard_map/while/body/eval_jaxpr/ppermute | solution.py:19
  261.7 9.2 %collective-permute-start = (bf16[48,1152]{1,0:T(8,128)(2,1)S(1)}, bf16[48,1152]{1,0:T(8,128)(2,1)S(1)}, u32[]{:S(2)}, u32[]{:S(2)}) collective-permute-start(bf16[48,1152]{1,0:T(8,128)(2,1)S(1)} %copy.54), channel_id=1, source_target_pairs={{0,64},{64,128},{128,192},{192,256},{256,320},{320,384},{384,448},... | collective-permute-start | bytes 331784 | tf_op jit(solution)/shard_map/while/body/eval_jaxpr/ppermute | solution.py:19
  264.7 9.4 %collective-permute-start.1 = (f32[48,1152]{1,0:T(8,128)S(1)}, f32[48,1152]{1,0:T(8,128)S(1)}, u32[]{:S(2)}, u32[]{:S(2)}) collective-permute-start(f32[48,1152]{1,0:T(8,128)S(1)} %fusion.57), channel_id=1, source_target_pairs={{0,64},{64,128},{128,192},{192,256},{256,320},{320,384},{384,448},... | collective-permute-start | bytes 663560 | tf_op jit(solution)/shard_map/while/body/eval_jaxpr/ppermute | solution.py:19
  274.0 9.2 %collective-permute-start = (bf16[48,1152]{1,0:T(8,128)(2,1)S(1)}, bf16[48,1152]{1,0:T(8,128)(2,1)S(1)}, u32[]{:S(2)}, u32[]{:S(2)}) collective-permute-start(bf16[48,1152]{1,0:T(8,128)(2,1)S(1)} %copy.54), channel_id=1, source_target_pairs={{0,64},{64,128},{128,192},{192,256},{256,320},{320,384},{384,448},... | collective-permute-start | bytes 331784 | tf_op jit(solution)/shard_map/while/body/eval_jaxpr/ppermute | solution.py:19
  277.0 9.4 %collective-permute-start.1 = (f32[48,1152]{1,0:T(8,128)S(1)}, f32[48,1152]{1,0:T(8,128)S(1)}, u32[]{:S(2)}, u32[]{:S(2)}) collective-permute-start(f32[48,1152]{1,0:T(8,128)S(1)} %fusion.57), channel_id=1, source_target_pairs={{0,64},{64,128},{128,192},{192,256},{256,320},{320,384},{384,448},... | collective-permute-start | bytes 663560 | tf_op jit(solution)/shard_map/while/body/eval_jaxpr/ppermute | solution.py:19
  286.3 9.2 %collective-permute-start = (bf16[48,1152]{1,0:T(8,128)(2,1)S(1)}, bf16[48,1152]{1,0:T(8,128)(2,1)S(1)}, u32[]{:S(2)}, u32[]{:S(2)}) collective-permute-start(bf16[48,1152]{1,0:T(8,128)(2,1)S(1)} %copy.54), channel_id=1, source_target_pairs={{0,64},{64,128},{128,192},{192,256},{256,320},{320,384},{384,448},... | collective-permute-start | bytes 331784 | tf_op jit(solution)/shard_map/while/body/eval_jaxpr/ppermute | solution.py:19
  289.3 9.4 %collective-permute-start.1 = (f32[48,1152]{1,0:T(8,128)S(1)}, f32[48,1152]{1,0:T(8,128)S(1)}, u32[]{:S(2)}, u32[]{:S(2)}) collective-permute-start(f32[48,1152]{1,0:T(8,128)S(1)} %fusion.57), channel_id=1, source_target_pairs={{0,64},{64,128},{128,192},{192,256},{256,320},{320,384},{384,448},... | collective-permute-start | bytes 663560 | tf_op jit(solution)/shard_map/while/body/eval_jaxpr/ppermute | solution.py:19
  298.7 9.2 %collective-permute-start = (bf16[48,1152]{1,0:T(8,128)(2,1)S(1)}, bf16[48,1152]{1,0:T(8,128)(2,1)S(1)}, u32[]{:S(2)}, u32[]{:S(2)}) collective-permute-start(bf16[48,1152]{1,0:T(8,128)(2,1)S(1)} %copy.54), channel_id=1, source_target_pairs={{0,64},{64,128},{128,192},{192,256},{256,320},{320,384},{384,448},... | collective-permute-start | bytes 331784 | tf_op jit(solution)/shard_map/while/body/eval_jaxpr/ppermute | solution.py:19
  301.6 9.4 %collective-permute-start.1 = (f32[48,1152]{1,0:T(8,128)S(1)}, f32[48,1152]{1,0:T(8,128)S(1)}, u32[]{:S(2)}, u32[]{:S(2)}) collective-permute-start(f32[48,1152]{1,0:T(8,128)S(1)} %fusion.57), channel_id=1, source_target_pairs={{0,64},{64,128},{128,192},{192,256},{256,320},{320,384},{384,448},... | collective-permute-start | bytes 663560 | tf_op jit(solution)/shard_map/while/body/eval_jaxpr/ppermute | solution.py:19
  311.0 9.2 %collective-permute-start = (bf16[48,1152]{1,0:T(8,128)(2,1)S(1)}, bf16[48,1152]{1,0:T(8,128)(2,1)S(1)}, u32[]{:S(2)}, u32[]{:S(2)}) collective-permute-start(bf16[48,1152]{1,0:T(8,128)(2,1)S(1)} %copy.54), channel_id=1, source_target_pairs={{0,64},{64,128},{128,192},{192,256},{256,320},{320,384},{384,448},... | collective-permute-start | bytes 331784 | tf_op jit(solution)/shard_map/while/body/eval_jaxpr/ppermute | solution.py:19
  313.9 9.4 %collective-permute-start.1 = (f32[48,1152]{1,0:T(8,128)S(1)}, f32[48,1152]{1,0:T(8,128)S(1)}, u32[]{:S(2)}, u32[]{:S(2)}) collective-permute-start(f32[48,1152]{1,0:T(8,128)S(1)} %fusion.57), channel_id=1, source_target_pairs={{0,64},{64,128},{128,192},{192,256},{256,320},{320,384},{384,448},... | collective-permute-start | bytes 663560 | tf_op jit(solution)/shard_map/while/body/eval_jaxpr/ppermute | solution.py:19
  323.3 9.2 %collective-permute-start = (bf16[48,1152]{1,0:T(8,128)(2,1)S(1)}, bf16[48,1152]{1,0:T(8,128)(2,1)S(1)}, u32[]{:S(2)}, u32[]{:S(2)}) collective-permute-start(bf16[48,1152]{1,0:T(8,128)(2,1)S(1)} %copy.54), channel_id=1, source_target_pairs={{0,64},{64,128},{128,192},{192,256},{256,320},{320,384},{384,448},... | collective-permute-start | bytes 331784 | tf_op jit(solution)/shard_map/while/body/eval_jaxpr/ppermute | solution.py:19
  326.2 9.4 %collective-permute-start.1 = (f32[48,1152]{1,0:T(8,128)S(1)}, f32[48,1152]{1,0:T(8,128)S(1)}, u32[]{:S(2)}, u32[]{:S(2)}) collective-permute-start(f32[48,1152]{1,0:T(8,128)S(1)} %fusion.57), channel_id=1, source_target_pairs={{0,64},{64,128},{128,192},{192,256},{256,320},{320,384},{384,448},... | collective-permute-start | bytes 663560 | tf_op jit(solution)/shard_map/while/body/eval_jaxpr/ppermute | solution.py:19
  335.6 9.2 %collective-permute-start = (bf16[48,1152]{1,0:T(8,128)(2,1)S(1)}, bf16[48,1152]{1,0:T(8,128)(2,1)S(1)}, u32[]{:S(2)}, u32[]{:S(2)}) collective-permute-start(bf16[48,1152]{1,0:T(8,128)(2,1)S(1)} %copy.54), channel_id=1, source_target_pairs={{0,64},{64,128},{128,192},{192,256},{256,320},{320,384},{384,448},... | collective-permute-start | bytes 331784 | tf_op jit(solution)/shard_map/while/body/eval_jaxpr/ppermute | solution.py:19
  338.5 9.4 %collective-permute-start.1 = (f32[48,1152]{1,0:T(8,128)S(1)}, f32[48,1152]{1,0:T(8,128)S(1)}, u32[]{:S(2)}, u32[]{:S(2)}) collective-permute-start(f32[48,1152]{1,0:T(8,128)S(1)} %fusion.57), channel_id=1, source_target_pairs={{0,64},{64,128},{128,192},{192,256},{256,320},{320,384},{384,448},... | collective-permute-start | bytes 663560 | tf_op jit(solution)/shard_map/while/body/eval_jaxpr/ppermute | solution.py:19
  347.9 9.2 %collective-permute-start = (bf16[48,1152]{1,0:T(8,128)(2,1)S(1)}, bf16[48,1152]{1,0:T(8,128)(2,1)S(1)}, u32[]{:S(2)}, u32[]{:S(2)}) collective-permute-start(bf16[48,1152]{1,0:T(8,128)(2,1)S(1)} %copy.54), channel_id=1, source_target_pairs={{0,64},{64,128},{128,192},{192,256},{256,320},{320,384},{384,448},... | collective-permute-start | bytes 331784 | tf_op jit(solution)/shard_map/while/body/eval_jaxpr/ppermute | solution.py:19
  350.8 9.4 %collective-permute-start.1 = (f32[48,1152]{1,0:T(8,128)S(1)}, f32[48,1152]{1,0:T(8,128)S(1)}, u32[]{:S(2)}, u32[]{:S(2)}) collective-permute-start(f32[48,1152]{1,0:T(8,128)S(1)} %fusion.57), channel_id=1, source_target_pairs={{0,64},{64,128},{128,192},{192,256},{256,320},{320,384},{384,448},... | collective-permute-start | bytes 663560 | tf_op jit(solution)/shard_map/while/body/eval_jaxpr/ppermute | solution.py:19
  360.2 9.2 %collective-permute-start = (bf16[48,1152]{1,0:T(8,128)(2,1)S(1)}, bf16[48,1152]{1,0:T(8,128)(2,1)S(1)}, u32[]{:S(2)}, u32[]{:S(2)}) collective-permute-start(bf16[48,1152]{1,0:T(8,128)(2,1)S(1)} %copy.54), channel_id=1, source_target_pairs={{0,64},{64,128},{128,192},{192,256},{256,320},{320,384},{384,448},... | collective-permute-start | bytes 331784 | tf_op jit(solution)/shard_map/while/body/eval_jaxpr/ppermute | solution.py:19
  363.1 9.4 %collective-permute-start.1 = (f32[48,1152]{1,0:T(8,128)S(1)}, f32[48,1152]{1,0:T(8,128)S(1)}, u32[]{:S(2)}, u32[]{:S(2)}) collective-permute-start(f32[48,1152]{1,0:T(8,128)S(1)} %fusion.57), channel_id=1, source_target_pairs={{0,64},{64,128},{128,192},{192,256},{256,320},{320,384},{384,448},... | collective-permute-start | bytes 663560 | tf_op jit(solution)/shard_map/while/body/eval_jaxpr/ppermute | solution.py:19
  372.5 9.2 %collective-permute-start = (bf16[48,1152]{1,0:T(8,128)(2,1)S(1)}, bf16[48,1152]{1,0:T(8,128)(2,1)S(1)}, u32[]{:S(2)}, u32[]{:S(2)}) collective-permute-start(bf16[48,1152]{1,0:T(8,128)(2,1)S(1)} %copy.54), channel_id=1, source_target_pairs={{0,64},{64,128},{128,192},{192,256},{256,320},{320,384},{384,448},... | collective-permute-start | bytes 331784 | tf_op jit(solution)/shard_map/while/body/eval_jaxpr/ppermute | solution.py:19
  375.5 9.4 %collective-permute-start.1 = (f32[48,1152]{1,0:T(8,128)S(1)}, f32[48,1152]{1,0:T(8,128)S(1)}, u32[]{:S(2)}, u32[]{:S(2)}) collective-permute-start(f32[48,1152]{1,0:T(8,128)S(1)} %fusion.57), channel_id=1, source_target_pairs={{0,64},{64,128},{128,192},{192,256},{256,320},{320,384},{384,448},... | collective-permute-start | bytes 663560 | tf_op jit(solution)/shard_map/while/body/eval_jaxpr/ppermute | solution.py:19
  384.8 1.8 copy-start.6
where the time goes:
time: 393 us; the launch traced here: 387 us
  waiting for transfers between devices  198 us (50%)
  starting transfers between devices  103 us (26%)
  matrix products  36.8 us (9%)
  local copies, waits for them, and re-layouts  34.3 us (9%)
  other arithmetic  12.8 us (3%)
    all_to_all x1, waiting for transfers between devices, local(): lax.all_to_all(patches[0, 0], 'dp', split_axis=0, concat_axis=0, tiled=True)  103 us
    ppermute x32, waiting for transfers between devices, from_behind(): return lax.ppermute(value, axis, pairs)  95.1 us
    ppermute x32, starting transfers between devices, from_behind(): return lax.ppermute(value, axis, pairs)  76.6 us
    all_to_all x1, starting transfers between devices, local(): lax.all_to_all(patches[0, 0], 'dp', split_axis=0, concat_axis=0, tiled=True)  25.9 us
  transfers between devices with their start and end apart: 33, of which 31 were waited for; matrix products, arithmetic and copies ran while one was open for 7% of the time, Pallas kernels for 0%

commit v1 on v0

v1 whole, which is shorter than its diff:
```python
import functools

import jax
import jax.numpy as jnp
from jax import lax
from jax.experimental import pallas as pl
from jax.experimental.pallas import tpu as pltpu
from jax.sharding import PartitionSpec as P

HEADS = 8
HEAD_DIM = 72
SUBGROUP = 16

logit_scale = 16.0
logit_bias = -4.0
epsilon = 1e-06

NT = (((1,), (1,)), ((), ()))
MESH = pl.DeviceIdType.MESH
STEP_GROUPS = 2
PIECE = 16
LABEL_BASE = 32


def column_of(row):
    n = row.shape[1]
    eye = lax.broadcasted_iota(jnp.int32, (n, n), 0) == lax.broadcasted_iota(jnp.int32, (n, n), 1)
    return jnp.sum(jnp.where(eye, row, jnp.zeros_like(row)), axis=1, keepdims=True)


def row_of(column):
    n = column.shape[0]
    eye = lax.broadcasted_iota(jnp.int32, (n, n), 0) == lax.broadcasted_iota(jnp.int32, (n, n), 1)
    return jnp.sum(jnp.where(eye, column, jnp.zeros_like(column)), axis=0, keepdims=True)


def halves(values):
    high = values.astype(jnp.bfloat16)
    low = (values - high.astype(jnp.float32)).astype(jnp.bfloat16)
    return jnp.concatenate([high, low], axis=0)


def split_dot(values, other):
    rows = values.shape[0]
    both = jnp.dot(halves(values), other, preferred_element_type=jnp.float32)
    return both[:rows] + both[rows:]


def attend_kernel(
    patch_hbm, counts_ref, wt_hbm, wo_hbm, out_ref,
    patch_ref, wt_ref, wo_ref, normed_ref, packed_ref, mean_ref, pool_ref, wide_ref, sent_ref, arrived_ref,
    load_sems, send_sem, recv_sem,
):
    cap, dests, width = patch_ref.shape
    inner = HEADS * HEAD_DIM
    rows = cap * SUBGROUP
    groups = dests // SUBGROUP
    images = out_ref.shape[0]
    half = sent_ref.shape[2]
    me = lax.axis_index("dp")

    loads = [pltpu.make_async_copy(patch_hbm, patch_ref, load_sems.at[0])]
    for p in range(3):
        span = pl.ds(p * inner, inner)
        loads.append(pltpu.make_async_copy(wt_hbm.at[span], wt_ref.at[span], load_sems.at[1 + p]))
    loads.append(pltpu.make_async_copy(wo_hbm, wo_ref, load_sems.at[4]))
    for load in loads:
        load.start()

    barrier = pltpu.get_barrier_semaphore()

    def greet(step, carry):
        pl.semaphore_signal(barrier, inc=1, device_id={"dp": lax.rem(me + step, dests)}, device_id_type=MESH)
        return carry

    lax.fori_loop(1, dests, greet, 0)

    lengths_row = counts_ref[pl.ds(me, 1), :]
    id_row = lax.broadcasted_iota(jnp.int32, (SUBGROUP, dests), 1)
    id_column = lax.broadcasted_iota(jnp.int32, (SUBGROUP, dests), 0)
    order = [lax.rem(lax.div(me, SUBGROUP) + step, groups) for step in (2, 1, 3, 0)[4 - groups :]]
    lengths = [
        jnp.sum(jnp.where(id_row == id_column + g * SUBGROUP, lengths_row, 0), axis=1, keepdims=True) for g in order
    ]
    inverse_lengths = [1.0 / jnp.maximum(length, 1).astype(jnp.float32) for length in lengths]

    loads[0].wait()
    for k, g in enumerate(order):
        total = jnp.zeros((SUBGROUP, width), jnp.float32)
        for r in range(cap):
            block = patch_ref[r, pl.ds(pl.multiple_of(g * SUBGROUP, SUBGROUP), SUBGROUP), :].astype(jnp.float32)
            centred = block - jnp.mean(block, axis=-1, keepdims=True)
            spread = jnp.mean(centred * centred, axis=-1, keepdims=True)
            start = k * rows + r * SUBGROUP
            normed_ref[start : start + SUBGROUP, :] = (centred * lax.rsqrt(spread + epsilon)).astype(jnp.bfloat16)
            total = total + jnp.where(lengths[k] > r, block, 0.0)
        mean_ref[k * SUBGROUP : (k + 1) * SUBGROUP, :] = total * inverse_lengths[k]

    for p in range(3):
        loads[1 + p].wait()
        packed_ref[p] = lax.dot_general(
            normed_ref[...], wt_ref[p * inner : (p + 1) * inner, :], NT, preferred_element_type=jnp.float32
        ).astype(jnp.bfloat16)
    loads[4].wait()

    query_id = lax.broadcasted_iota(jnp.int32, (rows, rows), 0)
    key_id = lax.broadcasted_iota(jnp.int32, (rows, rows), 1)
    same_image = query_id % SUBGROUP == key_id % SUBGROUP
    lane_image = lax.broadcasted_iota(jnp.int32, (SUBGROUP, rows), 1) % SUBGROUP
    pick = lax.broadcasted_iota(jnp.int32, (SUBGROUP, rows), 0) == lane_image
    head_of = lax.broadcasted_iota(jnp.int32, (HEADS, 1, inner), 2)
    head_start = lax.broadcasted_iota(jnp.int32, (HEADS, 1, inner), 0) * HEAD_DIM
    head_mask = ((head_of >= head_start) & (head_of < head_start + HEAD_DIM)).astype(jnp.float32)
    column_id = lax.broadcasted_iota(jnp.int32, (1, inner), 1)

    def pool_group(k):
        key_lengths = jnp.sum(jnp.where(pick, lengths[k], 0), axis=0, keepdims=True)
        query_lengths = jnp.concatenate([lengths[k]] * cap, axis=0)
        query_live = query_id[:, :1] // SUBGROUP < query_lengths
        usable = same_image & (key_id // SUBGROUP < key_lengths) & query_live
        query_share = jnp.concatenate([inverse_lengths[k]] * cap, axis=0)
        group_rows = slice(k * rows, (k + 1) * rows)
        picked = []
        for h in range(HEADS):
            low = h * HEAD_DIM // 128 * 128
            high = min(-(-(h + 1) * HEAD_DIM // 128) * 128, inner)
            window = (column_id[:, low:high] >= h * HEAD_DIM) & (column_id[:, low:high] < (h + 1) * HEAD_DIM)
            queries = packed_ref[0, group_rows, low:high] * window.astype(jnp.bfloat16)
            keys = packed_ref[1, group_rows, low:high]
            scores = lax.dot_general(queries, keys, NT, preferred_element_type=jnp.float32) * HEAD_DIM ** (-0.5)
            raised = jnp.where(usable, jnp.exp(scores), 0.0)
            denominators = jnp.sum(raised, axis=-1, keepdims=True)
            weights = raised * jnp.where(query_live, query_share / denominators, 0.0)
            picked.append(jnp.sum(weights.reshape(cap, SUBGROUP, rows), axis=0))
        stacked = jnp.concatenate(picked, axis=0).astype(jnp.bfloat16)
        mixed = jnp.dot(stacked, packed_ref[2, group_rows, :], preferred_element_type=jnp.float32)
        return jnp.sum(mixed.reshape(HEADS, SUBGROUP, inner) * head_mask, axis=0)

    per_step = STEP_GROUPS
    for first in range(0, groups, per_step):
        members = range(first, min(first + per_step, groups))
        for k in members:
            pool_ref[k * SUBGROUP : (k + 1) * SUBGROUP, :] = pool_group(k)
        span = slice(first * SUBGROUP, (members[-1] + 1) * SUBGROUP)
        result = mean_ref[span, :] + split_dot(pool_ref[span, :], wo_ref[...])
        wide_ref[span, 0, :] = result[:, :half]
        filler = jnp.zeros((result.shape[0], 2 * half - width), jnp.float32)
        wide_ref[span, 1, :] = jnp.concatenate([result[:, half:], filler], axis=1)
        if first == 0:
            pl.semaphore_wait(barrier, dests - 1)
        for k in members:
            base = order[k] * SUBGROUP
            sent_ref[pl.ds(base, SUBGROUP)] = wide_ref[k * SUBGROUP : (k + 1) * SUBGROUP].astype(jnp.bfloat16)

            def send(step, carry, base=base):
                to = base + lax.rem(me + step, SUBGROUP)
                pltpu.make_async_remote_copy(
                    sent_ref.at[to], arrived_ref.at[me], send_sem, recv_sem, device_id={"dp": to}, device_id_type=MESH
                ).start()
                return carry

            lax.fori_loop(1 if k == groups - 1 else 0, SUBGROUP, send, 0)
    arrived_ref[me] = sent_ref[me]

    lane = lax.broadcasted_iota(jnp.int32, (dests, dests), 1)
    sublane = lax.broadcasted_iota(jnp.int32, (dests, dests), 0)
    intake = jnp.sum(jnp.where(lane == me, counts_ref[...], 0), axis=1, keepdims=True)
    living = (intake > 0).astype(jnp.int32)
    living_row = row_of(living)
    ranking_row = jnp.sum(jnp.where(sublane < lane, living, 0), axis=0, keepdims=True)
    image_id = lax.broadcasted_iota(jnp.int32, (images, dests), 0)
    chooser = ((ranking_row == image_id) & (living_row > 0)).astype(jnp.bfloat16)

    pltpu.make_async_remote_copy(
        sent_ref.at[pl.ds(0, dests - 1)], arrived_ref.at[pl.ds(0, dests - 1)], send_sem, recv_sem,
        device_id={"dp": lax.rem(me + 1, dests)}, device_id_type=MESH,
    ).wait()
    wide_ref[...] = arrived_ref[...].astype(jnp.float32)
    for low, high, lane_half in ((0, half, 0), (half, width, 1)):
        values = wide_ref[:, lane_half, : high - low].astype(jnp.bfloat16)
        chosen = jnp.dot(chooser, values, preferred_element_type=jnp.float32)
        out_ref[:, low:high] = chosen.astype(out_ref.dtype)


def attend(patch_rows, count_table, w_qkv_t, w_out, images):
    cap, dests, width = patch_rows.shape
    inner = HEADS * HEAD_DIM
    half = -(-width // 256) * 128
    vmem = pl.BlockSpec(memory_space=pltpu.VMEM)
    hbm = pl.BlockSpec(memory_space=pl.ANY)
    return pl.pallas_call(
        attend_kernel,
        out_shape=jax.ShapeDtypeStruct((images, width), jnp.bfloat16),
        in_specs=[hbm, vmem, hbm, hbm],
        out_specs=vmem,
        scratch_shapes=[
            pltpu.VMEM((cap, dests, width), jnp.bfloat16),
            pltpu.VMEM(w_qkv_t.shape, jnp.bfloat16),
            pltpu.VMEM(w_out.shape, jnp.bfloat16),
            pltpu.VMEM((cap * dests, width), jnp.bfloat16),
            pltpu.VMEM((3, cap * dests, inner), jnp.bfloat16),
            pltpu.VMEM((dests, width), jnp.float32),
            pltpu.VMEM((dests, inner), jnp.float32),
            pltpu.VMEM((dests, 2, half), jnp.float32),
            pltpu.VMEM((dests, 2, half), jnp.bfloat16),
            pltpu.VMEM((dests, 2, half), jnp.bfloat16),
            pltpu.SemaphoreType.DMA((5,)),
            pltpu.SemaphoreType.DMA,
            pltpu.SemaphoreType.DMA,
        ],
        compiler_params=pltpu.CompilerParams(
            collective_id=0, has_side_effects=True, vmem_limit_bytes=56 * 2**20
        ),
        cost_estimate=pl.CostEstimate(flops=5 * 10**9, bytes_accessed=8 * 10**6, transcendentals=10**6),
        name="attend",
    )(patch_rows, count_table, w_qkv_t, w_out)


def inverse_norms(values):
    return lax.rsqrt(jnp.sum(values * values, axis=-1, keepdims=True) + epsilon)


def pair_terms(own, own_scale, others, matching):
    others_scale = row_of(inverse_norms(others.astype(jnp.float32)))
    products = lax.dot_general(own, others, NT, preferred_element_type=jnp.float32)
    logits = logit_scale * (products * own_scale * others_scale) + logit_bias
    sign = jnp.where(matching, 1.0, -1.0)
    margins = -sign * logits
    slopes = -sign / (1.0 + jnp.exp(-margins))
    return margins, slopes * others_scale


def tangent(own, own_scale, gradient):
    unit = own.astype(jnp.float32) * own_scale
    return (gradient - unit * jnp.sum(unit * gradient, axis=-1, keepdims=True)) * own_scale


def contrast_kernel(
    img_ref, payload_hbm, text_ref, label_ref, loss_ref, img_grad_ref, text_grad_ref,
    texts_ref, gathered_ref, load_sem, send_sems, recv_sems,
):
    blocks, images, width = gathered_ref.shape
    me = lax.axis_index("blk")
    sibling = me + 1 - 2 * lax.rem(me, 2)

    def across(block):
        return block + 2 - 4 * lax.rem(lax.div(block, 2), 2)

    def mate(block):
        return block + 1 - 2 * lax.rem(block, 2)

    beside = across(me)
    right, left, opposite = (lax.rem(me + 4 * step, blocks) for step in (1, 3, 2))

    load = pltpu.make_async_copy(payload_hbm, texts_ref, load_sem)
    load.start()
    barrier = pltpu.get_barrier_semaphore()
    for neighbour in (sibling, beside, right, left):
        pl.semaphore_signal(barrier, inc=1, device_id={"blk": neighbour}, device_id_type=MESH)
    gathered_ref[me] = img_ref[...]

    pieces = images // PIECE
    started = []

    def put(stage, c, block, to):
        span = pl.ds(c * PIECE, PIECE)
        place = gathered_ref.at[block, span]
        k = stage * pieces + c
        copy = pltpu.make_async_remote_copy(
            img_ref.at[span] if block is me else place, place, send_sems.at[k], recv_sems.at[k],
            device_id={"blk": to}, device_id_type=MESH,
        )
        copy.start()
        started.append(copy)
        return copy

    own = img_ref[...]
    own_scale = inverse_norms(own.astype(jnp.float32))
    text = text_ref[...]
    text_scale = inverse_norms(text.astype(jnp.float32))
    label_column = column_of(label_ref[...])
    batch = 4
    wide = batch * images
    lane_id = lax.broadcasted_iota(jnp.int32, (images, wide), 1)
    text_id = me * images + lax.broadcasted_iota(jnp.int32, (images, wide), 0)

    def image_batch(q):
        others = texts_ref[batch * q : batch * (q + 1), :images, :].reshape(wide, width)
        margins, weights = pair_terms(own, own_scale, others, label_column == lane_id + q * wide)
        losses = jnp.maximum(margins, 0.0) + jnp.log1p(jnp.exp(-jnp.abs(margins)))
        gradient = split_dot(weights, others)
        if q == 0:
            img_grad_ref[...] = gradient
            return losses
        img_grad_ref[...] += gradient
        return losses

    def text_batch(head, is_first):
        first = lax.div(head, batch) * batch
        others = gathered_ref[pl.ds(first, batch)].reshape(wide, width)
        labels = []
        for i in range(batch):
            tail = texts_ref[first + i, images : images + 16, :images].astype(jnp.float32)
            labels.append(tail[0:1] * LABEL_BASE + tail[1:2])
        matching = jnp.concatenate(labels, axis=1).astype(jnp.int32) == text_id
        _, weights = pair_terms(text, text_scale, others, matching)
        gradient = split_dot(weights, others)
        if is_first:
            text_grad_ref[...] = gradient
        else:
            text_grad_ref[...] += gradient

    each = range(pieces)
    pl.semaphore_wait(barrier, 4)
    to_right = [put(0, c, me, right) for c in each]
    to_left = [put(1, c, me, left) for c in each]
    to_beside = [put(2, c, me, beside) for c in each]
    to_sibling = [put(3, c, me, sibling) for c in each]
    load.wait()
    losses = image_batch(0)

    sibling_waits = []
    beside_right, beside_left, opposite_own = [], [], []
    for c in each:
        to_beside[c].wait_recv()
        beside_right.append(put(4, c, beside, right))
        beside_left.append(put(5, c, beside, left))
        to_right[c].wait_recv()
        to_left[c].wait_recv()
        opposite_own.append(put(6, c, right, left) if c == 1 else put(6, c, left, right))
        sibling_waits.append(put(7, c, beside, sibling))
        sibling_waits.append(put(8, c, left, sibling))
        sibling_waits.append(put(9, c, right, sibling))
        if c + 1 < blocks // batch:
            losses = losses + image_batch(c + 1)
    for q in range(pieces + 1, blocks // batch):
        losses = losses + image_batch(q)

    opposite_beside = []
    for c in each:
        beside_right[c].wait_recv()
        beside_left[c].wait_recv()
        opposite_beside.append(put(10, c, across(left), right) if c == 1 else put(10, c, across(right), left))
        sibling_waits.append(put(11, c, across(left), sibling))
        sibling_waits.append(put(12, c, across(right), sibling))

    for copy in to_sibling:
        copy.wait_recv()
    for copy in sibling_waits[0::3][:pieces]:
        copy.wait_recv()
    text_batch(me, True)
    for c in each:
        opposite_own[c].wait_recv()
        last_own = put(13, c, opposite, sibling)
        opposite_beside[c].wait_recv()
        last_beside = put(14, c, across(opposite), sibling)
        started_last = (last_own, last_beside)
        sibling_waits.extend(started_last)
    for copy in sibling_waits[1 : 3 * pieces : 3] + sibling_waits[2 : 3 * pieces : 3]:
        copy.wait_recv()
    for copy in sibling_waits[3 * pieces : 5 * pieces]:
        copy.wait_recv()
    text_batch(left, False)
    text_batch(right, False)
    loss_ref[...] = row_of(jnp.sum(losses, axis=1, keepdims=True))
    img_grad_ref[...] = tangent(own, own_scale, logit_scale * img_grad_ref[...])
    for copy in sibling_waits[5 * pieces :]:
        copy.wait_recv()
    text_batch(opposite, False)
    text_grad_ref[...] = tangent(text, text_scale, logit_scale * text_grad_ref[...])
    for copy in started:
        copy.wait_send()


def contrast(own_images, payload, own_texts, labels):
    images, width = own_images.shape
    blocks = payload.shape[0]
    copies = 15 * (images // PIECE)
    vmem = pl.BlockSpec(memory_space=pltpu.VMEM)
    hbm = pl.BlockSpec(memory_space=pl.ANY)
    return pl.pallas_call(
        contrast_kernel,
        out_shape=(
            jax.ShapeDtypeStruct((1, images), jnp.float32),
            jax.ShapeDtypeStruct((images, width), jnp.float32),
            jax.ShapeDtypeStruct((images, width), jnp.float32),
        ),
        in_specs=[vmem, hbm, vmem, vmem],
        out_specs=(vmem,) * 3,
        scratch_shapes=[
            pltpu.VMEM(payload.shape, jnp.bfloat16),
            pltpu.VMEM((blocks, images, width), jnp.bfloat16),
            pltpu.SemaphoreType.DMA,
            pltpu.SemaphoreType.DMA((copies,)),
            pltpu.SemaphoreType.DMA((copies,)),
        ],
        compiler_params=pltpu.CompilerParams(
            collective_id=1, has_side_effects=True, vmem_limit_bytes=56 * 2**20
        ),
        cost_estimate=pl.CostEstimate(flops=10**9, bytes_accessed=4 * 10**6, transcendentals=10**5),
        name="contrast",
    )(own_images, payload, own_texts, labels)


def local(patches, counts, w_qkv, w_out, text_rows, labels):
    own_texts = text_rows[0]
    images, width = own_texts.shape
    count_table = counts[0]
    coded = jnp.concatenate([labels // LABEL_BASE, labels % LABEL_BASE], axis=0).astype(jnp.bfloat16)
    tail = jnp.pad(coded, ((0, 16 - coded.shape[0]), (0, width - images)))
    payload = lax.all_gather(jnp.concatenate([own_texts, tail], axis=0), "blk")
    patch_rows = jnp.transpose(patches[0, 0], (1, 0, 2))
    own_images = attend(patch_rows, count_table, w_qkv.T, w_out, images)
    losses, d_pooled, d_texts = contrast(own_images, payload, own_texts, labels)
    return (losses, d_pooled[None], d_texts[None])


def solution(mesh):
    in_specs = (
        P("blk", "dp", None, None, None),
        P("blk", None, None),
        P(),
        P(),
        P("dp", "blk", None),
        P("dp", "blk"),
    )
    out_specs = (P("dp", "blk"), P("dp", "blk", None), P("dp", "blk", None))
    return jax.shard_map(local, mesh=mesh, in_specs=in_specs, out_specs=out_specs, check_vma=False)
```

time: 393 us -> 97 us (0.25); the launches traced: 387 us -> 96.6 us
  waiting for transfers between devices: 198 us -> 11.6 us
  starting transfers between devices: 103 us -> 0.04 us
  Pallas kernels: 0 us -> 64.3 us
  matrix products: 36.8 us -> 0 us
  local copies, waits for them, and re-layouts: 34.3 us -> 4.44 us
  between operations: 0.93 us -> 14 us
  other arithmetic: 12.8 us -> 2.25 us
    all_to_all x1 -> x0, waiting for transfers between devices: 103 us -> none  [local(): lax.all_to_all(patches[0, 0], 'dp', split_axis=0, concat_axis=0, tiled=True)]
    ppermute x32 -> x0, waiting for transfers between devices: 95.1 us -> none  [from_behind(): return lax.ppermute(value, axis, pairs)]
    ppermute x32 -> x0, starting transfers between devices: 76.6 us -> none  [from_behind(): return lax.ppermute(value, axis, pairs)]
    pallas_call x0 -> x2, Pallas kernels: none -> 64.3 us  [the longest x1 45.8 us: attend(): pl.pallas_call(attend_kernel, out_shape=jax.ShapeDtypeStruct((images, wid...]
    dot_general x52 -> x0, matrix products: 36.8 us -> none  [the longest x16 7.8 us: one_turn(): jnp.einsum('ij,jd->id', slopes, text_unit, precision=highest)]
    all_to_all x1 -> x0, starting transfers between devices: 25.9 us -> none  [local(): lax.all_to_all(patches[0, 0], 'dp', split_axis=0, concat_axis=0, tiled=True)]
    all_gather x0 -> x1, waiting for transfers between devices: none -> 11.6 us  [local(): payload = lax.all_gather(jnp.concatenate([own_texts, tail], axis=0), 'blk')]
    reduce_sum x25 -> x0, other arithmetic: 8.56 us -> none  [the longest x1 2.92 us: pool_blocks(): totals = jnp.sum(result * kept_rows, axis=1)]
  transfers between devices with their start and end apart: 33 -> 1, of which waited for: 31 -> 1; matrix products, arithmetic and copies ran while one was open for 7% -> 0% of each run, Pallas kernels for 0% -> 47%
where the time goes in v1:
time: 97 us; the launch traced here: 96.6 us
  Pallas kernels  64.3 us (66%)
  between operations  14 us (14%)
  waiting for transfers between devices  11.6 us (12%)
  local copies, waits for them, and re-layouts  4.44 us (5%)
  other arithmetic  2.25 us (2%)
    pallas_call x1, Pallas kernels, attend(): pl.pallas_call(attend_kernel, out_shape=jax.ShapeDtypeStruct((images, wid...  45.8 us
    pallas_call x1, Pallas kernels, contrast(): pl.pallas_call(contrast_kernel, out_shape=(jax.ShapeDtypeStruct((1, image...  18.5 us
    all_gather x1, waiting for transfers between devices, local(): payload = lax.all_gather(jnp.concatenate([own_texts, tail], axis=0), 'blk')  11.6 us
    unnamed x3, local copies, waits for them, and re-layouts  4.44 us
  transfers between devices with their start and end apart: 1, of which 1 were waited for; matrix products, arithmetic and copies ran while one was open for 0% of the time, Pallas kernels for 47%

profile of v1, /device:TPU:1, one launch (start us, length us, event | category | flops | bytes accessed | tf_op | source)
XLA Modules:
  0.0 96.6 jit_solution(6294611447611503767)
XLA Ops:
  7.2 0.0 all-gather.3.cloned.1.call-start
  7.2 0.7 fusion.7
  7.9 1.6 %pad_maximum_fusion = bf16[64,1152]{1,0:T(8,128)(2,1)} fusion(bf16[16,1152]{1,0:T(8,128)(2,1)S(1)} %fusion.5, bf16[48,1152]{1,0:T(8,128)(2,1)} %bitcast.11), kind=kLoop, calls=%fused_computation | loop fusion | flops 294912 | bytes 294912 | tf_op jit(solution)/shard_map/concatenate | solution.py:411
  9.5 0.0 all-gather.3.cloned.1.call-update
  9.5 45.8 %attend.1.img_ref = bf16[48,1152]{1,0:T(8,128)(2,1)} custom-call(bf16[12,64,1152]{2,1,0:T(8,128)(2,1)} %bitcast.15, s32[64,64]{1,0:T(8,128)} %bitcast.16, bf16[1728,1152]{1,0:T(8,128)(2,1)} %bitcast.13, bf16[576,1152]{1,0:T(8,128)(2,1)} %wo_hbm.1), custom_call_target="tpu_custom_call" | custom-call | flops 5000000000 | bytes 8000000 | tf_op jit(solution)/shard_map/attend/pallas_call | solution.py:191
  55.3 11.6 %all-gather.3.cloned.1.call-done = bf16[1024,1152]{1,0:T(8,128)(2,1)} async-done(((bf16[64,1152]{1,0:T(8,128)(2,1)}), bf16[1024,1152]{1,0:T(8,128)(2,1)}) %all-gather.3.cloned.1.call-update) | async-done | bytes 2359312 | tf_op jit(solution)/shard_map/all_gather | solution.py:411
  66.9 18.5 %contrast.1 = (f32[1,48]{1,0:T(1,128)}, f32[48,1152]{1,0:T(8,128)}, f32[48,1152]{1,0:T(8,128)}) custom-call(bf16[48,1152]{1,0:T(8,128)(2,1)} %attend.1.img_ref, bf16[16,64,1152]{2,1,0:T(8,128)(2,1)} %bitcast.14, bf16[48,1152]{1,0:T(8,128)(2,1)} %bitcast.12, s32[1,48]{1,0:T(1,128)} %label_ref.1), custom_call_target="tpu_custom_call" | custom-call | flops 1000000000 | bytes 4000000 | tf_op jit(solution)/shard_map/contrast/pallas_call | solution.py:381
  85.3 1.2 %copy.12 = f32[1,48]{1,0:T(1,128)} copy(f32[1,48]{1,0:T(1,128)} %get-tuple-element.14) | data formatting | bytes 384
  86.5 1.6 %copy.13 = f32[1,48,1152]{2,1,0:T(8,128)} copy(f32[1,48,1152]{2,1,0:T(8,128)} %bitcast.10) | data formatting | bytes 442368
  88.2 1.6 %copy.14 = f32[1,48,1152]{2,1,0:T(8,128)} copy(f32[1,48,1152]{2,1,0:T(8,128)} %bitcast.9) | data formatting | bytes 442368
  (1 shorter events, 0.0 us)
Async XLA Ops:
  7.2 59.7 %all-gather.3.cloned.1.call-start = ((), (), s32[]{:S(2)}) async-start(), calls=%async_computation | async-start | bytes 2506752 | tf_op jit(solution)/shard_map/all_gather | solution.py:411
Sparse Core Ops, SparseCore 0:
  11.3 55.5 all-gather.2
